TPU v7x, 32 devices: a whole 2x2x4 slice. The times are simulated.
32 devices in a mesh: groups: 2 (over y), adapter: 4 (over z), tensor: 2 (over x), sub: 2 (over core).
Axes of the slice: x: 2, y: 2, z: 4, core: 2. Of those that a mesh axis runs over, the one named last changes fastest.
Arguments:
- hidden: bfloat16 [2048, 4, 8192], P(('groups', 'adapter'), None, 'tensor'), parts along dimension 0, may hold values from -6 to 6
- request_adapter: int32 [2048], P(('groups', 'adapter')), parts along dimension 0, may hold values from 0 to 63, as said below
- value_matrix: bfloat16 [8192, 1024], P('tensor', 'sub'), may hold values from -0.0625 to 0.0625
- adapter_down: bfloat16 [64, 8192, 64], P('adapter', ('tensor', 'sub')), may hold values from -0.0625 to 0.0625
- adapter_up: bfloat16 [64, 64, 1024], P('adapter', None, 'sub'), may hold values from -0.75 to 0.75
Outputs:
- projected: bfloat16 [2048, 4, 1024], P(('groups', 'adapter'), None, 'sub'), parts along dimension 0
There are 2 independent parts, one for each index of `groups`. A program takes and returns all parts, laid end to end along the dimension named above; an argument that names none is the same for every part. Nothing has to cross between parts.
Inputs may be any that keep to these rules, and one draw needn't show every extreme that they name: The adapter of request r is held by index request_adapter[r] // 16 of adapter. Among the 256 requests of one index of adapter (aligned blocks), at most 128 have adapters held by the same index; in every draw some index holds the adapters of exactly 128 requests of every block.
All inputs are finite; a program needn't handle non-finite values.
Results may differ from a plain program's by a relative error of at most 0.005.
Values may be sent and summed in bfloat16 or wider, within the bound.
A program may use at most 128 MiB of HBM per device.

v0:
```python
import jax
import jax.numpy as jnp
from jax import lax
from jax.sharding import PartitionSpec as P

adapter_scale = 0.5


def widen_rows(reduced_rows, up_table, group_lengths):
    high_part = reduced_rows.astype(jnp.bfloat16)
    low_part = (reduced_rows - high_part.astype(jnp.float32)).astype(jnp.bfloat16)
    first = lax.ragged_dot(high_part, up_table, group_lengths, preferred_element_type=jnp.float32)
    second = lax.ragged_dot(low_part, up_table, group_lengths, preferred_element_type=jnp.float32)
    return first + second


def local(hidden, request_adapter, value_matrix, adapter_down, adapter_up):
    owner_count = lax.axis_size("adapter")
    req_count, decode_count, feature_count = hidden.shape
    adapter_number = adapter_down.shape[0]
    width_halved = adapter_down.shape[1]
    column_number = adapter_up.shape[2]
    capacity = 2 * req_count // owner_count
    sub_index = lax.axis_index("sub")
    owner_of = request_adapter // adapter_number
    local_id = request_adapter % adapter_number
    owner_hits = (owner_of[:, None] == jnp.arange(owner_count)[None, :]).astype(jnp.int32)
    earlier = jnp.cumsum(owner_hits, axis=0) - owner_hits
    slot_of = jnp.sum(earlier * owner_hits, axis=1)
    destination = owner_of * capacity + slot_of
    feature_half = lax.dynamic_slice_in_dim(hidden, sub_index * width_halved, width_halved, 2)
    outgoing = jnp.zeros((owner_count * capacity, decode_count, width_halved), hidden.dtype)
    outgoing = (
        outgoing.at[destination]
        .set(feature_half)
        .reshape(owner_count, capacity, decode_count, width_halved)
    )
    labels = jnp.full((owner_count * capacity,), -1, jnp.int32).at[destination].set(local_id)
    labels = labels.reshape(owner_count, capacity)
    rows_in = lax.all_to_all(outgoing, "adapter", split_axis=0, concat_axis=0, tiled=True)
    tag_ids = lax.all_to_all(labels, "adapter", split_axis=0, concat_axis=0, tiled=True)
    source_count, slot_count = tag_ids.shape
    place_total = source_count * slot_count
    flat_tags = jnp.maximum(tag_ids.reshape(place_total), 0)
    ordering = jnp.argsort(flat_tags, stable=True)
    restore = jnp.argsort(ordering, stable=True)
    ordered_rows = rows_in.reshape(place_total, decode_count, width_halved)[ordering]
    ordered_rows = ordered_rows.reshape(place_total * decode_count, width_halved)
    tag_hits = (flat_tags[:, None] == jnp.arange(adapter_number)[None, :]).astype(jnp.int32)
    group_lengths = jnp.sum(tag_hits, axis=0) * decode_count
    reduced_rows = lax.ragged_dot(
        ordered_rows, adapter_down, group_lengths, preferred_element_type=jnp.float32
    )
    reduced_rows = lax.psum(reduced_rows, "sub")
    update_rows = widen_rows(reduced_rows, adapter_up, group_lengths).reshape(
        place_total, decode_count, column_number
    )
    update_rows = update_rows[restore].reshape(
        source_count, slot_count, decode_count, column_number
    )
    returned = lax.all_to_all(update_rows, "adapter", split_axis=0, concat_axis=0, tiled=True)
    returned = returned.reshape(owner_count * capacity, decode_count, returned.shape[3])
    returned_rows = returned[destination]
    plain_rows = jnp.einsum("rsf,fc->rsc", hidden, value_matrix, preferred_element_type=jnp.float32)
    merged_output = plain_rows + adapter_scale * returned_rows
    summed = lax.psum(merged_output, "tensor")
    return summed.astype(jnp.bfloat16)


def solution(mesh):
    return jax.shard_map(
        local,
        mesh=mesh,
        in_specs=(
            P(("groups", "adapter"), None, "tensor"),
            P(("groups", "adapter")),
            P("tensor", "sub"),
            P("adapter", ("tensor", "sub"), None),
            P("adapter", None, "sub"),
        ),
        out_specs=P(("groups", "adapter"), None, "sub"),
        check_vma=False,
    )
```

profile of v0, /device:TPU:1, one launch (start us, length us, event | category | flops | bytes accessed | tf_op | source)
XLA Modules:
  0.0 557.2 jit_solution(9915325921973105734)
XLA Ops:
  6.5 0.7 and_select_fusion
  7.2 1.2 reduce-window.6
  8.5 0.1 copy.18
  8.9 2.0 scatter_custom_fusion.1
  10.8 5.4 all-to-all-start.1
  16.3 6.2 %constant_dynamic-slice_fusion = bf16[256,4,2048]{2,1,0:T(4,128)(2,1)} fusion(bf16[256,4,4096]{2,1,0:T(4,128)(2,1)} %param.5, s32[]{:T(128)S(6)} %select_n.28), kind=kLoop, calls=%fused_computation.37 | loop fusion | bytes 8388612 | tf_op jit(solution)/shard_map/dynamic_slice | solution.py:31
  22.5 7.5 %broadcast_in_dim.10 = bf16[512,4,2048]{2,1,0:T(4,128)(2,1)} broadcast(bf16[]{:T(256)} %constant.25.clone.1), dimensions={} | broadcast | bytes 8388610 | tf_op jit(solution)/shard_map/broadcast_in_dim | solution.py:32
  30.0 33.4 %scatter_fusion = bf16[512,4,2048]{2,1,0:T(4,128)(2,1)} fusion(bf16[512,4,2048]{2,1,0:T(4,128)(2,1)} %broadcast_in_dim.10, s32[256]{0:T(256)S(1)} %compare_select_fusion.2, bf16[256,4,2048]{2,1,0:T(4,128)(2,1)} %constant_dynamic-slice_fusion), kind=kCustom, calls=%fused_computation.3 | custom fusion | bytes 12583936 | tf_op jit(solution)/shard_map/scatter | solution.py:35
  63.4 5.7 %all-to-all-start = ((bf16[4,128,4,2048]{3,2,1,0:T(4,128)(2,1)}), bf16[4,128,4,2048]{3,2,1,0:T(4,128)(2,1)}, u32[]{:S(2)}, u32[]{:S(2)}) async-start(bf16[4,128,4,2048]{3,2,1,0:T(4,128)(2,1)} %bitcast.31), calls=%async_computation | async-start | bytes 16777216 | tf_op jit(solution)/shard_map/all_to_all | solution.py:40
  69.1 8.4 %copy.20 = bf16[16,2048,64]{2,1,0:T(8,128)(2,1)} copy(bf16[16,2048,64]{1,2,0:T(8,128)(2,1)} %param.8) | data formatting | bytes 8388608 | tf_op args[3]
  77.5 3.8 sort.31
  81.3 0.1 convert_reduce_fusion
  81.4 0.5 broadcast_multiply_fusion
  81.9 1.8 ragged-dot-metadata
  83.8 167.9 %all-to-all-done = bf16[4,128,4,2048]{3,2,1,0:T(4,128)(2,1)} async-done(((bf16[4,128,4,2048]{3,2,1,0:T(4,128)(2,1)}), bf16[4,128,4,2048]{3,2,1,0:T(4,128)(2,1)}, u32[]{:S(2)}, u32[]{:S(2)}) %all-to-all-start) | async-done | bytes 8388640 | tf_op jit(solution)/shard_map/all_to_all | solution.py:40
  251.7 20.6 %gather_fusion = bf16[512,4,2048]{2,1,0:T(4,128)(2,1)} fusion(bf16[512,4,2048]{2,1,0:T(4,128)(2,1)} %bitcast.7, s32[1024]{0:T(1024)S(1)} %pad_clamp_fusion.2), kind=kCustom, calls=%fused_computation | custom fusion | bytes 16779264 | tf_op jit(solution)/shard_map/gather | solution.py:47
  272.3 12.5 %reshape.51 = bf16[2048,2048]{1,0:T(8,128)(2,1)} reshape(bf16[512,4,2048]{2,1,0:T(4,128)(2,1)} %gather_fusion) | data formatting | bytes 16777216 | tf_op jit(solution)/shard_map/reshape | solution.py:48
  284.8 20.9 %ragged-dot-none.2 = f32[2048,64]{1,0:T(8,128)} custom-call(s32[1]{0:T(128)} %get-tuple-element.13, s32[17]{0:T(128)} %get-tuple-element.14, s32[23]{0:T(128)} %get-tuple-element.15, s32[23]{0:T(128)} %get-tuple-element.16, s32[1]{0:T(128)} %get-tuple-element.13, bf16[2048,2048]{1,0:T(8,128)(2,1)} %reshape.51, bf16[16,2048,64]{2,1,0:T(8,128)(2,1)} %copy.20), custom_call_target="tpu_custom_call" | custom-call | flops 536870912 | bytes 13107264 | tf_op jit(solution)/shard_map/ragged_dot_general/ragged-dot-none
  305.8 3.8 sort.32
  309.6 17.2 %all-reduce.3.cloned.1.call-done = f32[2048,64]{1,0:T(8,128)} async-done(((f32[2048,64]{1,0:T(8,128)}), f32[2048,64]{1,0:T(8,128)}) %all-reduce.3.cloned.1.call-update) | async-done | bytes 524304 | tf_op jit(solution)/shard_map/psum | solution.py:54
  326.8 2.6 subtract_convert_fusion
  329.4 15.8 %ragged-dot-none = f32[2048,512]{1,0:T(8,128)} custom-call(s32[1]{0:T(128)} %get-tuple-element.13, s32[17]{0:T(128)} %get-tuple-element.14, s32[23]{0:T(128)} %get-tuple-element.15, s32[23]{0:T(128)} %get-tuple-element.16, s32[1]{0:T(128)} %get-tuple-element.13, bf16[2048,64]{1,0:T(8,128)(2,1)} %get-tuple-element.21, bf16[16,64,512]{2,1,0:T(8,128)(2,1)} %param.9), custom_call_target="tpu_custom_call" | custom-call | flops 134217728 | bytes 5505088 | tf_op jit(solution)/shard_map/ragged_dot_general/ragged-dot-none
  345.2 15.6 %ragged-dot-none.1 = f32[2048,512]{1,0:T(8,128)} custom-call(s32[1]{0:T(128)} %get-tuple-element.13, s32[17]{0:T(128)} %get-tuple-element.14, s32[23]{0:T(128)} %get-tuple-element.15, s32[23]{0:T(128)} %get-tuple-element.16, s32[1]{0:T(128)} %get-tuple-element.13, bf16[2048,64]{1,0:T(8,128)(2,1)} %get-tuple-element.22, bf16[16,64,512]{2,1,0:T(8,128)(2,1)} %param.9), custom_call_target="tpu_custom_call" | custom-call | flops 134217728 | bytes 5505088 | tf_op jit(solution)/shard_map/ragged_dot_general/ragged-dot-none
  360.8 6.5 %add.39 = f32[2048,512]{1,0:T(8,128)} add(f32[2048,512]{1,0:T(8,128)} %ragged-dot-none.1, f32[2048,512]{1,0:T(8,128)} %ragged-dot-none) | non-fusion elementwise | flops 1048576 | bytes 12582912 | tf_op jit(solution)/shard_map/add | solution.py:14
  367.3 5.2 reshape.52
  372.5 7.1 %gather_fusion.1 = f32[512,4,512]{2,1,0:T(4,128)} fusion(f32[512,4,512]{2,1,0:T(4,128)} %reshape.52, s32[1024]{0:T(1024)S(1)} %pad_clamp_fusion.1), kind=kCustom, calls=%fused_computation.1 | custom fusion | bytes 8390656 | tf_op jit(solution)/shard_map/gather | solution.py:58
  379.6 6.4 %all-to-all-start.2 = ((f32[4,128,4,512]{3,2,1,0:T(4,128)}), f32[4,128,4,512]{3,2,1,0:T(4,128)}, u32[]{:S(2)}, u32[]{:S(2)}) async-start(f32[4,128,4,512]{3,2,1,0:T(4,128)} %bitcast.32), calls=%async_computation.2 | async-start | bytes 8388608 | tf_op jit(solution)/shard_map/all_to_all | solution.py:61
  386.0 92.8 %all-to-all-done.2 = f32[4,128,4,512]{3,2,1,0:T(4,128)} async-done(((f32[4,128,4,512]{3,2,1,0:T(4,128)}), f32[4,128,4,512]{3,2,1,0:T(4,128)}, u32[]{:S(2)}, u32[]{:S(2)}) %all-to-all-start.2) | async-done | bytes 4194336 | tf_op jit(solution)/shard_map/all_to_all | solution.py:61
  478.8 4.0 gather_fusion.2
  482.9 15.6 %fusion.3 = f32[256,4,512]{2,0,1:T(8,128)} fusion(f32[256,4,512]{2,1,0:T(4,128)S(1)} %gather_fusion.2, bf16[4096,512]{1,0:T(8,128)(2,1)} %param.7, bf16[256,4,4096]{2,1,0:T(4,128)(2,1)} %param.5), kind=kOutput, calls=%fused_computation.9 | convolution fusion | flops 4296015872 | bytes 16777216 | tf_op jit(solution)/shard_map/rsf,fc->rsc/dot_general | solution.py:64
  498.4 50.1 %all-reduce.4 = bf16[256,4,512]{2,0,1:T(8,128)(2,1)S(1)} all-reduce(f32[256,4,512]{2,0,1:T(8,128)} %fusion.3), channel_id=1, replica_groups=mesh['groups'=2,'adapter'=4,'tensor'=2,'sub'=2] {'tensor'}, use_global_device_ids=true, to_apply=%region_9.10 | all-reduce | flops 524288 | bytes 3145728 | tf_op jit(solution)/shard_map/psum | solution.py:66
  548.6 1.8 copy.22
  (19 shorter events, 0.4 us)
Async XLA Ops:
  10.8 52.5 %all-to-all-start.1 = ((s32[4,1,128]{2,1,0:T(1,128)}), s32[4,1,128]{2,1,0:T(1,128)S(1)}, u32[]{:S(2)}, u32[]{:S(2)}) async-start(s32[4,1,128]{2,1,0:T(1,128)} %bitcast.4), calls=%async_computation.1 | async-start | bytes 4096 | tf_op jit(solution)/shard_map/all_to_all | solution.py:41
  63.4 188.3 %all-to-all-start = ((bf16[4,128,4,2048]{3,2,1,0:T(4,128)(2,1)}), bf16[4,128,4,2048]{3,2,1,0:T(4,128)(2,1)}, u32[]{:S(2)}, u32[]{:S(2)}) async-start(bf16[4,128,4,2048]{3,2,1,0:T(4,128)(2,1)} %bitcast.31), calls=%async_computation | async-start | bytes 16777216 | tf_op jit(solution)/shard_map/all_to_all | solution.py:40
  69.1 257.7 %all-reduce.3.cloned.1.call-start = ((), (), s32[]{:S(2)}) async-start(), calls=%async_computation.3 | async-start | bytes 2097152 | tf_op jit(solution)/shard_map/psum | solution.py:54
  379.6 99.3 %all-to-all-start.2 = ((f32[4,128,4,512]{3,2,1,0:T(4,128)}), f32[4,128,4,512]{3,2,1,0:T(4,128)}, u32[]{:S(2)}, u32[]{:S(2)}) async-start(f32[4,128,4,512]{3,2,1,0:T(4,128)} %bitcast.32), calls=%async_computation.2 | async-start | bytes 8388608 | tf_op jit(solution)/shard_map/all_to_all | solution.py:61
Sparse Core Ops, SparseCore 0:
  305.9 20.8 all-reduce.2
where the time goes:
time: 564 us; the launch traced here: 557 us
  waiting for transfers between devices  278 us (49%)
  local copies, waits for them, and re-layouts  109 us (19%)
  Pallas kernels  54.2 us (10%)
  blocking collectives  50.1 us (9%)
  other arithmetic  19.4 us (3%)
  starting transfers between devices  17.6 us (3%)
  matrix products  15.6 us (3%)
  between operations  13.5 us (2%)
    all_to_all x1, waiting for transfers between devices, local(): lax.all_to_all(outgoing, 'adapter', split_axis=0, concat_axis=0, tiled=True)  168 us
    all_to_all x1, waiting for transfers between devices, local(): lax.all_to_all(update_rows, 'adapter', split_axis=0, concat_axis=0, tiled...  92.8 us
    another operation x3, Pallas kernels  52.4 us
    psum x1, blocking collectives, local(): summed = lax.psum(merged_output, 'tensor')  50.1 us
    scatter x1, local copies, waits for them, and re-layouts, local(): outgoing = outgoing.at[destination].set(feature_half).reshape(owner_count...  33.4 us
    gather x1, local copies, waits for them, and re-layouts, local(): rows_in.reshape(place_total, decode_count, width_halved)[ordering]  20.6 us
    psum x1, waiting for transfers between devices, local(): reduced_rows = lax.psum(reduced_rows, 'sub')  17.2 us
    dot_general x1, matrix products, local(): jnp.einsum('rsf,fc->rsc', hidden, value_matrix, preferred_element_type=jn...  15.6 us
  transfers between devices with their start and end apart: 4, of which 3 were waited for; matrix products, arithmetic and copies ran while one was open for 11% of the time, Pallas kernels for 0%

commit v1 on v0

--- a/solution.py
+++ b/solution.py
@@ -1,6 +1,10 @@
+import functools
+
 import jax
 import jax.numpy as jnp
 from jax import lax
+from jax.experimental import pallas as pl
+from jax.experimental.pallas import tpu as pltpu
 from jax.sharding import PartitionSpec as P
 
 adapter_scale = 0.5
@@ -14,7 +18,7 @@
     return first + second
 
 
-def local(hidden, request_adapter, value_matrix, adapter_down, adapter_up):
+def routed(hidden, request_adapter, value_matrix, adapter_down, adapter_up):
     owner_count = lax.axis_size("adapter")
     req_count, decode_count, feature_count = hidden.shape
     adapter_number = adapter_down.shape[0]
@@ -67,6 +71,297 @@
     return summed.astype(jnp.bfloat16)
 
 
+LAG = 2
+TILE = 256
+LANES = 128
+
+
+def kernel(dims, hid_in, val_in, down_in, up_in, key, out, hid, val, w, up, acc, base, base_out, base_in,
+           low_out, low_in, loc, zs, zr, ys, yr, xs, xr, bs, br, ls, lr):
+    z_count, pairs, rank, feats = dims
+    rows = acc.shape[0]
+    half = pairs // 2
+    x, y = lax.axis_index("tensor"), lax.axis_index("groups")
+    z, s = lax.axis_index("adapter"), lax.axis_index("sub")
+    quarter = up.shape[1] // 4
+    mine_q = pl.ds(pl.multiple_of((2 * x + y) * quarter, quarter), quarter)
+    other_q = pl.ds(pl.multiple_of((2 * x + 1 - y) * quarter, quarter), quarter)
+    mine_h = pl.ds(pl.multiple_of(x * 2 * quarter, quarter), 2 * quarter)
+    other_h = pl.ds(pl.multiple_of((1 - x) * 2 * quarter, quarter), 2 * quarter)
+    cols = pl.ds(pl.multiple_of(s * feats, LANES), feats)
+    to_y, to_x = {"groups": 1 - y}, {"tensor": 1 - x}
+    peers = [{"tensor": 1 - x}, {"sub": 1 - s}, {"tensor": 1 - x, "sub": 1 - s}]
+
+    def remote(src, dst, send, recv, dev):
+        return pltpu.make_async_remote_copy(
+            src_ref=src, dst_ref=dst, send_sem=send, recv_sem=recv,
+            device_id=dev, device_id_type=pl.DeviceIdType.MESH)
+
+    local_copies = [
+        pltpu.make_async_copy(hid_in, hid, loc.at[0]),
+        pltpu.make_async_copy(val_in, val, loc.at[1]),
+        pltpu.make_async_copy(down_in, w.at[z], loc.at[2]),
+        pltpu.make_async_copy(up_in, up.at[z], loc.at[3]),
+    ]
+    for copy in local_copies:
+        copy.start()
+
+    barrier = pltpu.get_barrier_semaphore()
+    for dev in peers + [to_y]:
+        pl.semaphore_signal(barrier, inc=1, device_id=dev, device_id_type=pl.DeviceIdType.MESH)
+
+    @pl.when(z > 0)
+    def _():
+        pl.semaphore_signal(barrier, inc=1, device_id={"adapter": z - 1}, device_id_type=pl.DeviceIdType.MESH)
+
+    @pl.when(z < z_count - 1)
+    def _():
+        pl.semaphore_signal(barrier, inc=1, device_id={"adapter": z + 1}, device_id_type=pl.DeviceIdType.MESH)
+
+    ends = (z == 0).astype(jnp.int32) + (z == z_count - 1).astype(jnp.int32)
+    pl.semaphore_wait(barrier, len(peers) + 3 - ends)
+
+    def owner_of(d, t):
+        return z - (1 - 2 * d) * t
+
+    def target_of(d):
+        return z + 1 - 2 * d
+
+    def inside(k):
+        return jnp.logical_and(k >= 0, k < z_count)
+
+    def z_up(d, t, owner, src=None):
+        ref = up.at[owner, mine_q]
+        return remote(ref if src is None else src, ref, zs.at[d, t, half], zr.at[d, t, half],
+                      {"adapter": target_of(d)})
+
+    def z_down(d, t, owner, c, src=None):
+        ref = w.at[owner, y * half + c]
+        return remote(ref if src is None else src, ref, zs.at[d, t, c], zr.at[d, t, c],
+                      {"adapter": target_of(d)})
+
+    def y_up(d, t, owner, rows_at):
+        ref = up.at[owner, rows_at]
+        return remote(ref, ref, ys.at[d, t, half], yr.at[d, t, half], to_y)
+
+    def y_down(d, t, owner, pair, c):
+        ref = w.at[owner, pair]
+        return remote(ref, ref, ys.at[d, t, c], yr.at[d, t, c], to_y)
+
+    def x_up(d, t, owner, rows_at):
+        ref = up.at[owner, rows_at]
+        return remote(ref, ref, xs.at[d, t], xr.at[d, t], to_x)
+
+    for d in range(2):
+        @pl.when(inside(target_of(d)))
+        def _(d=d):
+            z_up(d, 1, z, up_in.at[mine_q]).start()
+    for c in range(half):
+        for d in range(2):
+            @pl.when(inside(target_of(d)))
+            def _(d=d, c=c):
+                z_down(d, 1, z, c, down_in.at[y * half + c]).start()
+
+    for copy in local_copies:
+        copy.wait()
+
+    base_copy = remote(base_out, base_in, bs, br, to_x)
+
+    @pl.loop(0, rows // TILE)
+    def _(r):
+        at = pl.ds(pl.multiple_of(r * TILE, TILE), TILE)
+        got = jnp.dot(hid[at, :], val[...], preferred_element_type=jnp.float32)
+        base[at, :] = got
+        base_out[at, :] = got.astype(jnp.bfloat16)
+        acc[at, :] = jnp.zeros((TILE, LANES), jnp.float32)
+
+    base_copy.start()
+
+    def use(owner, pair):
+        @pl.loop(0, rows // TILE)
+        def _(r):
+            at = pl.ds(pl.multiple_of(r * TILE, TILE), TILE)
+            got = lax.dot_general(
+                hid[at, cols], w[owner, pair], (((1,), (1,)), ((), ())), preferred_element_type=jnp.float32)
+            acc[at, :] += jnp.where(key[at, :] == 2 * (owner * pairs + pair), got, 0.0)
+
+    @pl.loop(0, pairs)
+    def _(pair):
+        use(z, pair)
+
+    total = (z_count - 1) * half
+
+    @pl.loop(0, total + LAG)
+    def _(i):
+        @pl.when(i < total)
+        def _():
+            t, c = i // half + 1, i % half
+
+            @pl.loop(0, 2)
+            def _(d):
+                owner = owner_of(d, t)
+
+                @pl.when(inside(owner))
+                def _():
+                    @pl.when(c == 0)
+                    def _():
+                        z_up(d, t, owner).wait_recv()
+
+                        @pl.when(inside(target_of(d)))
+                        def _():
+                            z_up(d, t + 1, owner).start()
+
+                        y_up(d, t, owner, mine_q).start()
+
+                    z_down(d, t, owner, c).wait_recv()
+
+                    @pl.when(inside(target_of(d)))
+                    def _():
+                        z_down(d, t + 1, owner, c).start()
+
+                    y_down(d, t, owner, y * half + c, c).start()
+
+            @pl.loop(0, 2)
+            def _(d):
+                owner = owner_of(d, t)
+
+                @pl.when(inside(owner))
+                def _():
+                    use(owner, y * half + c)
+
+        @pl.when(i >= LAG)
+        def _():
+            t, c = (i - LAG) // half + 1, (i - LAG) % half
+
+            @pl.loop(0, 2)
+            def _(d):
+                owner = owner_of(d, t)
+
+                @pl.when(inside(owner))
+                def _():
+                    @pl.when(c == 0)
+                    def _():
+                        y_up(d, t, owner, other_q).wait_recv()
+                        x_up(d, t, owner, mine_h).start()
+
+                    y_down(d, t, owner, (1 - y) * half + c, c).wait_recv()
+                    use(owner, (1 - y) * half + c)
+
+    mid = rows // 2
+    lane = lax.broadcasted_iota(jnp.int32, (mid, LANES), 1)
+    top = acc[:mid, :] + pltpu.roll(acc[:mid, :], rank, 1)
+    bottom = acc[mid:, :] + pltpu.roll(acc[mid:, :], rank, 1)
+    packed = jnp.where(lane < rank, top, bottom)
+    low_out[...] = packed.astype(jnp.bfloat16)
+    low_copies = [remote(low_out, low_in.at[n], ls.at[n], lr.at[n], dev) for n, dev in enumerate(peers)]
+    for copy in low_copies:
+        copy.start()
+
+    @pl.loop(1, z_count)
+    def _(t):
+        @pl.loop(0, 2)
+        def _(d):
+            owner = owner_of(d, t)
+
+            @pl.when(inside(owner))
+            def _():
+                x_up(d, t, owner, other_h).wait_recv()
+                x_up(d, t, owner, mine_h).wait_send()
+                y_up(d, t, owner, mine_q).wait_send()
+
+                @pl.loop(0, half)
+                def _(c):
+                    y_down(d, t, owner, y * half + c, c).wait_send()
+
+            before = owner_of(d, t - 1)
+
+            @pl.when(jnp.logical_and(inside(before), inside(target_of(d))))
+            def _():
+                z_up(d, t, before).wait_send()
+
+                @pl.loop(0, half)
+                def _(c):
+                    z_down(d, t, before, c).wait_send()
+
+    base_copy.wait()
+    for copy in low_copies:
+        copy.wait()
+    packed = packed + low_in[0].astype(jnp.float32) + low_in[1].astype(jnp.float32) + low_in[2].astype(jnp.float32)
+    turned = pltpu.roll(packed, rank, 1)
+    acc[:mid, :] = jnp.where(lane < rank, packed, turned)
+    acc[mid:, :] = jnp.where(lane < rank, turned, packed)
+
+    @pl.loop(0, rows // TILE)
+    def _(r):
+        at = pl.ds(pl.multiple_of(r * TILE, TILE), TILE)
+        low, which = acc[at, :], key[at, :]
+        delta = jnp.zeros((TILE, out.shape[1]), jnp.float32)
+        for o in range(z_count):
+            spread = jnp.concatenate(
+                [jnp.where(which == 2 * (o * pairs + p), low, 0.0).astype(jnp.bfloat16) for p in range(pairs)], axis=1)
+            delta += jnp.dot(spread, up[o], preferred_element_type=jnp.float32)
+        sums = base[at, :] + base_in[at, :].astype(jnp.float32)
+        out[at, :] = (sums + adapter_scale * delta).astype(jnp.bfloat16)
+
+
+def gathered(hidden, request_adapter, value_matrix, adapter_down, adapter_up):
+    z_count = lax.axis_size("adapter")
+    reqs, steps, width = hidden.shape
+    adapters, feats, rank = adapter_down.shape
+    columns = adapter_up.shape[2]
+    rows, pairs = reqs * steps, adapters // 2
+    half = pairs // 2
+    down = adapter_down.transpose(0, 2, 1).reshape(pairs, 2 * rank, feats)
+    up = adapter_up.reshape(adapters * rank, columns)
+    key = jnp.repeat(request_adapter, steps)[:, None] - (jnp.arange(2 * rank, dtype=jnp.int32) // rank)[None, :]
+    bf, f32, dma = jnp.bfloat16, jnp.float32, pltpu.SemaphoreType.DMA
+    anywhere = pl.BlockSpec(memory_space=pl.ANY)
+    whole = pl.BlockSpec(memory_space=pltpu.VMEM)
+    out = pl.pallas_call(
+        functools.partial(kernel, (z_count, pairs, rank, feats)),
+        out_shape=jax.ShapeDtypeStruct((rows, columns), bf),
+        in_specs=[anywhere] * 4 + [whole],
+        out_specs=whole,
+        scratch_shapes=[
+            pltpu.VMEM((rows, width), bf),
+            pltpu.VMEM(value_matrix.shape, bf),
+            pltpu.VMEM((z_count, pairs, 2 * rank, feats), bf),
+            pltpu.VMEM((z_count, adapters * rank, columns), bf),
+            pltpu.VMEM((rows, 2 * rank), f32),
+            pltpu.VMEM((rows, columns), f32),
+            pltpu.VMEM((rows, columns), bf),
+            pltpu.VMEM((rows, columns), bf),
+            pltpu.VMEM((rows // 2, 2 * rank), bf),
+            pltpu.VMEM((3, rows // 2, 2 * rank), bf),
+            dma((4,)),
+            dma((2, z_count, half + 1)),
+            dma((2, z_count, half + 1)),
+            dma((2, z_count, half + 1)),
+            dma((2, z_count, half + 1)),
+            dma((2, z_count)),
+            dma((2, z_count)),
+            dma, dma,
+            dma((3,)),
+            dma((3,)),
+        ],
+        compiler_params=pltpu.CompilerParams(
+            collective_id=0, has_side_effects=True, vmem_limit_bytes=60 * 2 ** 20),
+        cost_estimate=pl.CostEstimate(flops=30 * 10 ** 9, bytes_accessed=20 * 10 ** 6, transcendentals=0),
+    )(hidden.reshape(rows, width), value_matrix, down, up, key)
+    return out.reshape(reqs, steps, columns)
+
+
+def local(hidden, request_adapter, value_matrix, adapter_down, adapter_up):
+    z_count = lax.axis_size("adapter")
+    reqs, steps, width = hidden.shape
+    maps = z_count * (adapter_down.size + adapter_up.size) * 2
+    rest = (hidden.size + value_matrix.size) * 2 + reqs * steps * adapter_up.shape[2] * 10
+    fits = maps + rest < 50 * 2 ** 20
+    if fits and lax.axis_size("tensor") == 2 and lax.axis_size("groups") == 2 and lax.axis_size("sub") == 2:
+        return gathered(hidden, request_adapter, value_matrix, adapter_down, adapter_up)
+    return routed(hidden, request_adapter, value_matrix, adapter_down, adapter_up)
+
+
 def solution(mesh):
     return jax.shard_map(
         local,

time: 564 us -> 215 us (0.38); the launches traced: 557 us -> 214 us
  waiting for transfers between devices: 278 us -> 0 us
  Pallas kernels: 54.2 us -> 198 us
  local copies, waits for them, and re-layouts: 109 us -> 15.5 us
  blocking collectives: 50.1 us -> 0 us
  other arithmetic: 19.4 us -> 1 us
  starting transfers between devices: 17.6 us -> 0 us
  matrix products: 15.6 us -> 0 us
  between operations: 13.5 us -> 0.02 us
    all_to_all x3 -> x0, waiting for transfers between devices: 261 us -> none  [the longest x1 168 us: local(): lax.all_to_all(outgoing, 'adapter', split_axis=0, concat_axis=0, tiled=True)]
    pallas_call x0 -> x1, Pallas kernels: none -> 198 us  [gathered(): pl.pallas_call(functools.partial(kernel, (z_count, pairs, rank, feats)),...]
    another operation x3 -> x0, Pallas kernels: 52.4 us -> none
    psum x1 -> x0, blocking collectives: 50.1 us -> none  [local(): summed = lax.psum(merged_output, 'tensor')]
    scatter x2 -> x0, local copies, waits for them, and re-layouts: 35.4 us -> none  [the longest x1 33.4 us: local(): outgoing = outgoing.at[destination].set(feature_half).reshape(owner_count...]
    gather x3 -> x0, local copies, waits for them, and re-layouts: 31.8 us -> none  [the longest x1 20.6 us: local(): rows_in.reshape(place_total, decode_count, width_halved)[ordering]]
    all_to_all x3 -> x0, starting transfers between devices: 17.5 us -> none  [the longest x1 6.43 us: local(): lax.all_to_all(update_rows, 'adapter', split_axis=0, concat_axis=0, tiled...]
    psum x1 -> x0, waiting for transfers between devices: 17.2 us -> none  [local(): reduced_rows = lax.psum(reduced_rows, 'sub')]
  transfers between devices with their start and end apart: 4 -> 0, of which waited for: 3 -> 0; matrix products, arithmetic and copies ran while one was open for 11% -> 0% of each run, Pallas kernels for 0% -> 0%
where the time goes in v1:
time: 215 us; the launch traced here: 214 us
  Pallas kernels  198 us (92%)
  local copies, waits for them, and re-layouts  15.5 us (7%)
    pallas_call x1, Pallas kernels, gathered(): pl.pallas_call(functools.partial(kernel, (z_count, pairs, rank, feats)),...  198 us
    reshape x1, local copies, waits for them, and re-layouts, gathered(): hidden.reshape(rows, width)  12.5 us

profile of v1, /device:TPU:1, one launch (start us, length us, event | category | flops | bytes accessed | tf_op | source)
XLA Modules:
  0.0 214.4 jit_solution(2327215583245227049)
XLA Ops:
  0.0 0.8 broadcast_in_dim.4
  0.8 0.1 sub.21
  0.9 1.0 broadcast_subtract_fusion.key
  1.9 12.5 %reshape.26.hid_in = bf16[1024,4096]{1,0:T(8,128)(2,1)} reshape(bf16[256,4,4096]{2,1,0:T(4,128)(2,1)} %param.5) | data formatting | bytes 16777216 | tf_op jit(solution)/shard_map/reshape | solution.py:350
  14.4 197.9 %shard_map.55 = bf16[1024,512]{1,0:T(8,128)(2,1)} custom-call(bf16[1024,4096]{1,0:T(8,128)(2,1)} %reshape.26.hid_in, bf16[4096,512]{1,0:T(8,128)(2,1)} %val_in.1, bf16[8,128,2048]{2,1,0:T(8,128)(2,1)} %bitcast.4, bf16[1024,512]{1,0:T(8,128)(2,1)} %bitcast.5, s32[1024,128]{1,0:T(8,128)} %broadcast_subtract_fusion.key), custom_call_target="tpu_custom_call" | custom-call | flops 30000001024 | bytes 20000000 | tf_op jit(solution)/shard_map/pallas_call | solution.py:320
  212.3 2.1 reshape.29
  (1 shorter events, 0.0 us)

commit v2 on v1

--- a/solution.py
+++ b/solution.py
@@ -71,16 +71,17 @@
     return summed.astype(jnp.bfloat16)
 
 
-LAG = 2
 TILE = 256
 LANES = 128
 
 
-def kernel(dims, hid_in, val_in, down_in, up_in, key, out, hid, val, w, up, acc, base, base_out, base_in,
-           low_out, low_in, loc, zs, zr, ys, yr, xs, xr, bs, br, ls, lr):
+def kernel(dims, hid_in, val_in, down_in, up_in, key, out, hid3, hid, hidy3, hidy, keyy, val, w, up, acc, accy, base,
+           base_out, base_in, low_out, low_in, loc, zs, zr, us, ur, xs, xr, hs, hr, bs, br, ls, lr):
     z_count, pairs, rank, feats = dims
     rows = acc.shape[0]
+    steps = hid3.shape[1]
     half = pairs // 2
+    tiles, step_rows = rows // TILE, TILE // steps
     x, y = lax.axis_index("tensor"), lax.axis_index("groups")
     z, s = lax.axis_index("adapter"), lax.axis_index("sub")
     quarter = up.shape[1] // 4
@@ -89,37 +90,43 @@
     mine_h = pl.ds(pl.multiple_of(x * 2 * quarter, quarter), 2 * quarter)
     other_h = pl.ds(pl.multiple_of((1 - x) * 2 * quarter, quarter), 2 * quarter)
     cols = pl.ds(pl.multiple_of(s * feats, LANES), feats)
+    my_half = pl.ds(y * half, half)
     to_y, to_x = {"groups": 1 - y}, {"tensor": 1 - x}
-    peers = [{"tensor": 1 - x}, {"sub": 1 - s}, {"tensor": 1 - x, "sub": 1 - s}]
+    peers = [{"tensor": 1 - x}, {"sub": 1 - s}, {"tensor": 1 - x, "sub": 1 - s},
+             {"groups": 1 - y}, {"groups": 1 - y, "tensor": 1 - x}, {"groups": 1 - y, "sub": 1 - s},
+             {"groups": 1 - y, "tensor": 1 - x, "sub": 1 - s}]
 
     def remote(src, dst, send, recv, dev):
         return pltpu.make_async_remote_copy(
             src_ref=src, dst_ref=dst, send_sem=send, recv_sem=recv,
             device_id=dev, device_id_type=pl.DeviceIdType.MESH)
 
+    def signal(dev, barrier):
+        pl.semaphore_signal(barrier, inc=1, device_id=dev, device_id_type=pl.DeviceIdType.MESH)
+
     local_copies = [
-        pltpu.make_async_copy(hid_in, hid, loc.at[0]),
+        pltpu.make_async_copy(hid_in, hid3, loc.at[0]),
         pltpu.make_async_copy(val_in, val, loc.at[1]),
-        pltpu.make_async_copy(down_in, w.at[z], loc.at[2]),
+        pltpu.make_async_copy(down_in.at[my_half], w.at[z], loc.at[2]),
         pltpu.make_async_copy(up_in, up.at[z], loc.at[3]),
     ]
     for copy in local_copies:
         copy.start()
 
     barrier = pltpu.get_barrier_semaphore()
-    for dev in peers + [to_y]:
-        pl.semaphore_signal(barrier, inc=1, device_id=dev, device_id_type=pl.DeviceIdType.MESH)
+    for dev in peers:
+        signal(dev, barrier)
 
     @pl.when(z > 0)
     def _():
-        pl.semaphore_signal(barrier, inc=1, device_id={"adapter": z - 1}, device_id_type=pl.DeviceIdType.MESH)
+        signal({"adapter": z - 1}, barrier)
 
     @pl.when(z < z_count - 1)
     def _():
-        pl.semaphore_signal(barrier, inc=1, device_id={"adapter": z + 1}, device_id_type=pl.DeviceIdType.MESH)
+        signal({"adapter": z + 1}, barrier)
 
     ends = (z == 0).astype(jnp.int32) + (z == z_count - 1).astype(jnp.int32)
-    pl.semaphore_wait(barrier, len(peers) + 3 - ends)
+    pl.semaphore_wait(barrier, len(peers) + 2 - ends)
 
     def owner_of(d, t):
         return z - (1 - 2 * d) * t
@@ -136,21 +143,23 @@
                       {"adapter": target_of(d)})
 
     def z_down(d, t, owner, c, src=None):
-        ref = w.at[owner, y * half + c]
+        ref = w.at[owner, c]
         return remote(ref if src is None else src, ref, zs.at[d, t, c], zr.at[d, t, c],
                       {"adapter": target_of(d)})
 
     def y_up(d, t, owner, rows_at):
         ref = up.at[owner, rows_at]
-        return remote(ref, ref, ys.at[d, t, half], yr.at[d, t, half], to_y)
-
-    def y_down(d, t, owner, pair, c):
-        ref = w.at[owner, pair]
-        return remote(ref, ref, ys.at[d, t, c], yr.at[d, t, c], to_y)
+        return remote(ref, ref, us.at[d, t], ur.at[d, t], to_y)
 
     def x_up(d, t, owner, rows_at):
         ref = up.at[owner, rows_at]
         return remote(ref, ref, xs.at[d, t], xr.at[d, t], to_x)
+
+    key_copy = remote(key, keyy, hs.at[tiles], hr.at[tiles], to_y)
+
+    def hidden_copy(r):
+        at = pl.ds(r * step_rows, step_rows)
+        return remote(hid_in.at[at, :, cols], hidy3.at[at], hs.at[r], hr.at[r], to_y)
 
     for d in range(2):
         @pl.when(inside(target_of(d)))
@@ -161,42 +170,59 @@
             @pl.when(inside(target_of(d)))
             def _(d=d, c=c):
                 z_down(d, 1, z, c, down_in.at[y * half + c]).start()
+    key_copy.start()
+    for r in range(tiles):
+        hidden_copy(r).start()
 
     for copy in local_copies:
         copy.wait()
 
     base_copy = remote(base_out, base_in, bs, br, to_x)
 
-    @pl.loop(0, rows // TILE)
+    def tile_at(r):
+        return pl.ds(pl.multiple_of(r * TILE, TILE), TILE)
+
+    @pl.loop(0, tiles)
     def _(r):
-        at = pl.ds(pl.multiple_of(r * TILE, TILE), TILE)
-        got = jnp.dot(hid[at, :], val[...], preferred_element_type=jnp.float32)
+        at = tile_at(r)
+        part = hid3[pl.ds(r * step_rows, step_rows)].reshape(TILE, hid.shape[1])
+        hid[at, :] = part
+        got = jnp.dot(part, val[...], preferred_element_type=jnp.float32)
         base[at, :] = got
         base_out[at, :] = got.astype(jnp.bfloat16)
         acc[at, :] = jnp.zeros((TILE, LANES), jnp.float32)
+        accy[at, :] = jnp.zeros((TILE, LANES), jnp.float32)
 
     base_copy.start()
 
-    def use(owner, pair):
-        @pl.loop(0, rows // TILE)
+    def add(part, which, total, at, owner):
+        maps = w[owner].reshape(half * LANES, feats)
+        got = lax.dot_general(part, maps, (((1,), (1,)), ((), ())), preferred_element_type=jnp.float32)
+        first = 2 * (owner * pairs + y * half)
+        ids = which[at, :] - first
+        more = total[at, :]
+        for p in range(half):
+            more += jnp.where(ids == 2 * p, got[:, p * LANES:(p + 1) * LANES], 0.0)
+        total[at, :] = more
+
+    def use(owner):
+        @pl.loop(0, tiles)
         def _(r):
-            at = pl.ds(pl.multiple_of(r * TILE, TILE), TILE)
-            got = lax.dot_general(
-                hid[at, cols], w[owner, pair], (((1,), (1,)), ((), ())), preferred_element_type=jnp.float32)
-            acc[at, :] += jnp.where(key[at, :] == 2 * (owner * pairs + pair), got, 0.0)
-
-    @pl.loop(0, pairs)
-    def _(pair):
-        use(z, pair)
-
-    total = (z_count - 1) * half
-
-    @pl.loop(0, total + LAG)
-    def _(i):
-        @pl.when(i < total)
-        def _():
-            t, c = i // half + 1, i % half
-
+            at = tile_at(r)
+            add(hid[at, cols], key, acc, at, owner)
+
+    def use_other(owner, r):
+        at = tile_at(r)
+        add(hidy[at, :], keyy, accy, at, owner)
+
+    use(z)
+
+    @pl.loop(1, z_count)
+    def _(t):
+        last = t == z_count - 1
+
+        @pl.loop(0, half)
+        def _(c):
             @pl.loop(0, 2)
             def _(d):
                 owner = owner_of(d, t)
@@ -219,41 +245,66 @@
                     def _():
                         z_down(d, t + 1, owner, c).start()
 
-                    y_down(d, t, owner, y * half + c, c).start()
-
+            @pl.when(jnp.logical_and(last, c == 1))
+            def _():
+                @pl.loop(1, z_count)
+                def _(k):
+                    @pl.loop(0, 2)
+                    def _(d):
+                        owner = owner_of(d, k)
+
+                        @pl.when(inside(owner))
+                        def _():
+                            y_up(d, k, owner, other_q).wait_recv()
+                            x_up(d, k, owner, mine_h).start()
+
+        @pl.loop(0, 2)
+        def _(d):
+            owner = owner_of(d, t)
+
+            @pl.when(inside(owner))
+            def _():
+                use(owner)
+
+        @pl.when(t == z_count - 2)
+        def _():
+            key_copy.wait_recv()
+
+            @pl.loop(0, tiles)
+            def _(r):
+                hidden_copy(r).wait_recv()
+                hidy[tile_at(r), :] = hidy3[pl.ds(r * step_rows, step_rows)].reshape(TILE, feats)
+
+                @pl.loop(0, z_count)
+                def _(owner):
+                    @pl.when(jnp.logical_and(owner - z < z_count - 1, z - owner < z_count - 1))
+                    def _():
+                        use_other(owner, r)
+
+        @pl.when(last)
+        def _():
             @pl.loop(0, 2)
             def _(d):
                 owner = owner_of(d, t)
 
                 @pl.when(inside(owner))
                 def _():
-                    use(owner, y * half + c)
-
-        @pl.when(i >= LAG)
-        def _():
-            t, c = (i - LAG) // half + 1, (i - LAG) % half
-
-            @pl.loop(0, 2)
-            def _(d):
-                owner = owner_of(d, t)
-
-                @pl.when(inside(owner))
-                def _():
-                    @pl.when(c == 0)
-                    def _():
-                        y_up(d, t, owner, other_q).wait_recv()
-                        x_up(d, t, owner, mine_h).start()
-
-                    y_down(d, t, owner, (1 - y) * half + c, c).wait_recv()
-                    use(owner, (1 - y) * half + c)
+                    @pl.loop(0, tiles)
+                    def _(r):
+                        use_other(owner, r)
 
     mid = rows // 2
     lane = lax.broadcasted_iota(jnp.int32, (mid, LANES), 1)
-    top = acc[:mid, :] + pltpu.roll(acc[:mid, :], rank, 1)
-    bottom = acc[mid:, :] + pltpu.roll(acc[mid:, :], rank, 1)
-    packed = jnp.where(lane < rank, top, bottom)
-    low_out[...] = packed.astype(jnp.bfloat16)
-    low_copies = [remote(low_out, low_in.at[n], ls.at[n], lr.at[n], dev) for n, dev in enumerate(peers)]
+
+    def pack(total):
+        top = total[:mid, :] + pltpu.roll(total[:mid, :], rank, 1)
+        bottom = total[mid:, :] + pltpu.roll(total[mid:, :], rank, 1)
+        return jnp.where(lane < rank, top, bottom)
+
+    low_out[1] = pack(accy).astype(jnp.bfloat16)
+    low_out[0] = pack(acc).astype(jnp.bfloat16)
+    low_copies = [
+        remote(low_out.at[0 if n < 3 else 1], low_in.at[n], ls.at[n], lr.at[n], dev) for n, dev in enumerate(peers)]
     for copy in low_copies:
         copy.start()
 
@@ -269,10 +320,6 @@
                 x_up(d, t, owner, mine_h).wait_send()
                 y_up(d, t, owner, mine_q).wait_send()
 
-                @pl.loop(0, half)
-                def _(c):
-                    y_down(d, t, owner, y * half + c, c).wait_send()
-
             before = owner_of(d, t - 1)
 
             @pl.when(jnp.logical_and(inside(before), inside(target_of(d))))
@@ -283,25 +330,31 @@
                 def _(c):
                     z_down(d, t, before, c).wait_send()
 
+    key_copy.wait_send()
+    for r in range(tiles):
+        hidden_copy(r).wait_send()
     base_copy.wait()
     for copy in low_copies:
         copy.wait()
-    packed = packed + low_in[0].astype(jnp.float32) + low_in[1].astype(jnp.float32) + low_in[2].astype(jnp.float32)
+    packed = pack(acc)
+    for n in range(len(peers)):
+        packed += low_in[n].astype(jnp.float32)
     turned = pltpu.roll(packed, rank, 1)
     acc[:mid, :] = jnp.where(lane < rank, packed, turned)
     acc[mid:, :] = jnp.where(lane < rank, turned, packed)
 
-    @pl.loop(0, rows // TILE)
+    @pl.loop(0, tiles)
     def _(r):
-        at = pl.ds(pl.multiple_of(r * TILE, TILE), TILE)
+        at = tile_at(r)
         low, which = acc[at, :], key[at, :]
-        delta = jnp.zeros((TILE, out.shape[1]), jnp.float32)
+        delta = jnp.zeros((TILE, base.shape[1]), jnp.float32)
         for o in range(z_count):
             spread = jnp.concatenate(
                 [jnp.where(which == 2 * (o * pairs + p), low, 0.0).astype(jnp.bfloat16) for p in range(pairs)], axis=1)
             delta += jnp.dot(spread, up[o], preferred_element_type=jnp.float32)
         sums = base[at, :] + base_in[at, :].astype(jnp.float32)
-        out[at, :] = (sums + adapter_scale * delta).astype(jnp.bfloat16)
+        result = (sums + adapter_scale * delta).astype(jnp.bfloat16)
+        out[pl.ds(r * step_rows, step_rows)] = result.reshape(step_rows, steps, base.shape[1])
 
 
 def gathered(hidden, request_adapter, value_matrix, adapter_down, adapter_up):
@@ -317,38 +370,44 @@
     bf, f32, dma = jnp.bfloat16, jnp.float32, pltpu.SemaphoreType.DMA
     anywhere = pl.BlockSpec(memory_space=pl.ANY)
     whole = pl.BlockSpec(memory_space=pltpu.VMEM)
-    out = pl.pallas_call(
+    return pl.pallas_call(
         functools.partial(kernel, (z_count, pairs, rank, feats)),
-        out_shape=jax.ShapeDtypeStruct((rows, columns), bf),
+        out_shape=jax.ShapeDtypeStruct((reqs, steps, columns), bf),
         in_specs=[anywhere] * 4 + [whole],
         out_specs=whole,
         scratch_shapes=[
+            pltpu.VMEM(hidden.shape, bf),
             pltpu.VMEM((rows, width), bf),
+            pltpu.VMEM((reqs, steps, feats), bf),
+            pltpu.VMEM((rows, feats), bf),
+            pltpu.VMEM((rows, 2 * rank), jnp.int32),
             pltpu.VMEM(value_matrix.shape, bf),
-            pltpu.VMEM((z_count, pairs, 2 * rank, feats), bf),
+            pltpu.VMEM((z_count, half, 2 * rank, feats), bf),
             pltpu.VMEM((z_count, adapters * rank, columns), bf),
+            pltpu.VMEM((rows, 2 * rank), f32),
             pltpu.VMEM((rows, 2 * rank), f32),
             pltpu.VMEM((rows, columns), f32),
             pltpu.VMEM((rows, columns), bf),
             pltpu.VMEM((rows, columns), bf),
-            pltpu.VMEM((rows // 2, 2 * rank), bf),
-            pltpu.VMEM((3, rows // 2, 2 * rank), bf),
+            pltpu.VMEM((2, rows // 2, 2 * rank), bf),
+            pltpu.VMEM((7, rows // 2, 2 * rank), bf),
             dma((4,)),
-            dma((2, z_count, half + 1)),
-            dma((2, z_count, half + 1)),
             dma((2, z_count, half + 1)),
             dma((2, z_count, half + 1)),
             dma((2, z_count)),
             dma((2, z_count)),
+            dma((2, z_count)),
+            dma((2, z_count)),
+            dma((rows // TILE + 1,)),
+            dma((rows // TILE + 1,)),
             dma, dma,
-            dma((3,)),
-            dma((3,)),
+            dma((7,)),
+            dma((7,)),
         ],
         compiler_params=pltpu.CompilerParams(
             collective_id=0, has_side_effects=True, vmem_limit_bytes=60 * 2 ** 20),
         cost_estimate=pl.CostEstimate(flops=30 * 10 ** 9, bytes_accessed=20 * 10 ** 6, transcendentals=0),
-    )(hidden.reshape(rows, width), value_matrix, down, up, key)
-    return out.reshape(reqs, steps, columns)
+    )(hidden, value_matrix, down, up, key)
 
 
 def local(hidden, request_adapter, value_matrix, adapter_down, adapter_up):

time: 215 us -> 194 us (0.902)
  local copies, waits for them, and re-layouts: 15.5 us -> 3.44 us
  Pallas kernels: 198 us -> 190 us
    reshape x2 -> x0, local copies, waits for them, and re-layouts: 14.7 us -> none  [the longest x1 12.5 us: gathered(): hidden.reshape(rows, width)]
    pallas_call x1, Pallas kernels: 198 us -> 190 us  [gathered(): pl.pallas_call(functools.partial(kernel, (z_count, pairs, rank, feats)),...]
    unnamed x0 -> x1, local copies, waits for them, and re-layouts: none -> 2.56 us
where the time goes in v2:
time: 194 us
  Pallas kernels  190 us (98%)
  local copies, waits for them, and re-layouts  3.44 us (2%)
    pallas_call x1, Pallas kernels, gathered(): pl.pallas_call(functools.partial(kernel, (z_count, pairs, rank, feats)),...  190 us

profile of v2, /device:TPU:1, one launch (start us, length us, event | category | flops | bytes accessed | tf_op | source)
XLA Modules:
  0.0 194.2 jit_solution(11906720537128762019)
XLA Ops:
  0.0 0.8 broadcast_in_dim.4
  0.8 0.1 sub.21
  0.9 1.0 broadcast_subtract_fusion.key
  1.9 189.7 %shard_map.55 = bf16[256,4,512]{2,1,0:T(4,128)(2,1)} custom-call(bf16[256,4,4096]{2,1,0:T(4,128)(2,1)} %hid_in.1, bf16[4096,512]{1,0:T(8,128)(2,1)} %val_in.1, bf16[8,128,2048]{2,1,0:T(8,128)(2,1)} %bitcast.4, bf16[1024,512]{1,0:T(8,128)(2,1)} %bitcast.5, s32[1024,128]{1,0:T(8,128)} %broadcast_subtract_fusion.key), custom_call_target="tpu_custom_call" | custom-call | flops 30000001024 | bytes 20000000 | tf_op jit(solution)/shard_map/pallas_call | solution.py:373
  191.6 2.6 %copy.7 = bf16[256,4,512]{2,1,0:T(4,128)(2,1)} copy(bf16[256,4,512]{2,1,0:T(4,128)(2,1)} %shard_map.55) | data formatting | bytes 2097152
  (1 shorter events, 0.0 us)

commit v3 on v2

--- a/solution.py
+++ b/solution.py
@@ -76,7 +76,7 @@
 
 
 def kernel(dims, hid_in, val_in, down_in, up_in, key, out, hid3, hid, hidy3, hidy, keyy, val, w, up, acc, accy, base,
-           base_out, base_in, low_out, low_in, loc, zs, zr, us, ur, xs, xr, hs, hr, bs, br, ls, lr):
+           base_out, base_in, low_out, low_in, wown, hidr3, keyr, accr, own, back_out, back_in, rs, rr, loc, zs, zr, us, ur, xs, xr, hs, hr, bs, br, ls, lr):
     z_count, pairs, rank, feats = dims
     rows = acc.shape[0]
     steps = hid3.shape[1]
@@ -109,6 +109,7 @@
         pltpu.make_async_copy(val_in, val, loc.at[1]),
         pltpu.make_async_copy(down_in.at[my_half], w.at[z], loc.at[2]),
         pltpu.make_async_copy(up_in, up.at[z], loc.at[3]),
+        pltpu.make_async_copy(down_in.at[:, :, pl.ds(0, feats // 2)], wown, loc.at[4]),
     ]
     for copy in local_copies:
         copy.start()
@@ -146,6 +147,26 @@
         ref = w.at[owner, c]
         return remote(ref if src is None else src, ref, zs.at[d, t, c], zr.at[d, t, c],
                       {"adapter": target_of(d)})
+
+    fh = feats // 2
+
+    def end(k):
+        return jnp.logical_or(k == 0, k == z_count - 1)
+
+    server = jnp.logical_or(z == 1, z == z_count - 2)
+    partner = jnp.where(z == 0, 1, jnp.where(z == z_count - 1, z_count - 2, jnp.where(z == 1, 0, z_count - 1)))
+
+    def z_part(d, owner, c):
+        at = pl.ds(fh, fh)
+        return remote(down_in.at[y * half + c, :, at], w.at[owner, c, :, at], zs.at[d, 1, c], zr.at[d, 1, c],
+                      {"adapter": target_of(d)})
+
+    first_cols = pl.ds(pl.multiple_of(s * feats, LANES), fh)
+    route = [
+        remote(hid_in.at[:, :, first_cols], hidr3, rs.at[0], rr.at[0], {"adapter": partner}),
+        remote(key, keyr, rs.at[1], rr.at[1], {"adapter": partner}),
+    ]
+    route_back = remote(back_out, back_in, rs.at[2], rr.at[2], {"adapter": partner})
 
     def y_up(d, t, owner, rows_at):
         ref = up.at[owner, rows_at]
@@ -167,9 +188,19 @@
             z_up(d, 1, z, up_in.at[mine_q]).start()
     for c in range(half):
         for d in range(2):
-            @pl.when(inside(target_of(d)))
+            @pl.when(jnp.logical_and(inside(target_of(d)), jnp.logical_not(end(target_of(d)))))
             def _(d=d, c=c):
                 z_down(d, 1, z, c, down_in.at[y * half + c]).start()
+
+            @pl.when(end(target_of(d)))
+            def _(d=d, c=c):
+                z_part(d, z, c).start()
+
+    @pl.when(end(z))
+    def _():
+        for copy in route:
+            copy.start()
+
     key_copy.start()
     for r in range(tiles):
         hidden_copy(r).start()
@@ -192,28 +223,42 @@
         base_out[at, :] = got.astype(jnp.bfloat16)
         acc[at, :] = jnp.zeros((TILE, LANES), jnp.float32)
         accy[at, :] = jnp.zeros((TILE, LANES), jnp.float32)
+        accr[at, :] = jnp.zeros((TILE, LANES), jnp.float32)
 
     base_copy.start()
 
-    def add(part, which, total, at, owner):
-        maps = w[owner].reshape(half * LANES, feats)
+    def add(part, maps, which, total, at, first):
         got = lax.dot_general(part, maps, (((1,), (1,)), ((), ())), preferred_element_type=jnp.float32)
-        first = 2 * (owner * pairs + y * half)
-        ids = which[at, :] - first
+        ids = which[at, :] - 2 * first
         more = total[at, :]
         for p in range(half):
             more += jnp.where(ids == 2 * p, got[:, p * LANES:(p + 1) * LANES], 0.0)
         total[at, :] = more
 
+    late_cols = pl.ds(pl.multiple_of(s * feats + fh, LANES), fh)
+
+    def meet(rows_ref, all_cols, cut_cols, which, total, owner, r):
+        at = tile_at(r)
+        first = owner * pairs + y * half
+        cut = jnp.logical_and(end(z), owner == partner)
+
+        @pl.when(cut)
+        def _():
+            maps = w[owner, :, :, fh:].reshape(half * LANES, fh)
+            add(rows_ref[at, cut_cols], maps, which, total, at, first)
+
+        @pl.when(jnp.logical_not(cut))
+        def _():
+            maps = w[owner].reshape(half * LANES, feats)
+            add(rows_ref[at, all_cols], maps, which, total, at, first)
+
     def use(owner):
         @pl.loop(0, tiles)
         def _(r):
-            at = tile_at(r)
-            add(hid[at, cols], key, acc, at, owner)
+            meet(hid, cols, late_cols, key, acc, owner, r)
 
     def use_other(owner, r):
-        at = tile_at(r)
-        add(hidy[at, :], keyy, accy, at, owner)
+        meet(hidy, pl.ds(0, feats), pl.ds(fh, fh), keyy, accy, owner, r)
 
     use(z)
 
@@ -239,7 +284,15 @@
 
                         y_up(d, t, owner, mine_q).start()
 
-                    z_down(d, t, owner, c).wait_recv()
+                    cut = jnp.logical_and(t == 1, end(z))
+
+                    @pl.when(cut)
+                    def _():
+                        z_part(d, owner, c).wait_recv()
+
+                    @pl.when(jnp.logical_not(cut))
+                    def _():
+                        z_down(d, t, owner, c).wait_recv()
 
                     @pl.when(inside(target_of(d)))
                     def _():
@@ -302,7 +355,29 @@
         return jnp.where(lane < rank, top, bottom)
 
     low_out[1] = pack(accy).astype(jnp.bfloat16)
-    low_out[0] = pack(acc).astype(jnp.bfloat16)
+    own[...] = pack(acc)
+
+    @pl.when(server)
+    def _():
+        for copy in route:
+            copy.wait_recv()
+
+        @pl.loop(0, tiles)
+        def _(r):
+            part = hidr3[pl.ds(r * step_rows, step_rows)].reshape(TILE, fh)
+            for h in range(2):
+                maps = wown[h * half:(h + 1) * half].reshape(half * LANES, fh)
+                add(part, maps, keyr, accr, tile_at(r), z * pairs + h * half)
+
+        back_out[...] = pack(accr).astype(jnp.bfloat16)
+        route_back.start()
+
+    @pl.when(end(z))
+    def _():
+        route_back.wait_recv()
+        own[...] += back_in[...].astype(jnp.float32)
+
+    low_out[0] = own[...].astype(jnp.bfloat16)
     low_copies = [
         remote(low_out.at[0 if n < 3 else 1], low_in.at[n], ls.at[n], lr.at[n], dev) for n, dev in enumerate(peers)]
     for copy in low_copies:
@@ -328,7 +403,24 @@
 
                 @pl.loop(0, half)
                 def _(c):
-                    z_down(d, t, before, c).wait_send()
+                    cut = jnp.logical_and(t == 1, end(target_of(d)))
+
+                    @pl.when(cut)
+                    def _():
+                        z_part(d, before, c).wait_send()
+
+                    @pl.when(jnp.logical_not(cut))
+                    def _():
+                        z_down(d, t, before, c).wait_send()
+
+    @pl.when(server)
+    def _():
+        route_back.wait_send()
+
+    @pl.when(end(z))
+    def _():
+        for copy in route:
+            copy.wait_send()
 
     key_copy.wait_send()
     for r in range(tiles):
@@ -336,7 +428,7 @@
     base_copy.wait()
     for copy in low_copies:
         copy.wait()
-    packed = pack(acc)
+    packed = own[...]
     for n in range(len(peers)):
         packed += low_in[n].astype(jnp.float32)
     turned = pltpu.roll(packed, rank, 1)
@@ -391,7 +483,16 @@
             pltpu.VMEM((rows, columns), bf),
             pltpu.VMEM((2, rows // 2, 2 * rank), bf),
             pltpu.VMEM((7, rows // 2, 2 * rank), bf),
-            dma((4,)),
+            pltpu.VMEM((pairs, 2 * rank, feats // 2), bf),
+            pltpu.VMEM((reqs, steps, feats // 2), bf),
+            pltpu.VMEM((rows, 2 * rank), jnp.int32),
+            pltpu.VMEM((rows, 2 * rank), f32),
+            pltpu.VMEM((rows // 2, 2 * rank), f32),
+            pltpu.VMEM((rows // 2, 2 * rank), bf),
+            pltpu.VMEM((rows // 2, 2 * rank), bf),
+            dma((3,)),
+            dma((3,)),
+            dma((5,)),
             dma((2, z_count, half + 1)),
             dma((2, z_count, half + 1)),
             dma((2, z_count)),
@@ -416,7 +517,7 @@
     maps = z_count * (adapter_down.size + adapter_up.size) * 2
     rest = (hidden.size + value_matrix.size) * 2 + reqs * steps * adapter_up.shape[2] * 10
     fits = maps + rest < 50 * 2 ** 20
-    if fits and lax.axis_size("tensor") == 2 and lax.axis_size("groups") == 2 and lax.axis_size("sub") == 2:
+    if fits and z_count >= 4 and lax.axis_size("tensor") == 2 and lax.axis_size("groups") == 2 and lax.axis_size("sub") == 2:
         return gathered(hidden, request_adapter, value_matrix, adapter_down, adapter_up)
     return routed(hidden, request_adapter, value_matrix, adapter_down, adapter_up)
 

time: 194 us -> 181 us (0.933)
  the two profiles are of different devices: /device:TPU:1 before, /device:TPU:15 now
where the time goes in v3:
time: 181 us
  Pallas kernels  177 us (98%)
  local copies, waits for them, and re-layouts  3.44 us (2%)
    pallas_call x1, Pallas kernels, gathered(): pl.pallas_call(functools.partial(kernel, (z_count, pairs, rank, feats)),...  177 us

profile of v3, /device:TPU:15, one launch (start us, length us, event | category | flops | bytes accessed | tf_op | source)
XLA Modules:
  0.0 181.0 jit_solution(8916628747834804360)
XLA Ops:
  0.0 0.8 broadcast_in_dim.4
  0.8 0.1 sub.21
  0.9 1.0 broadcast_subtract_fusion.key
  1.9 176.6 %shard_map.55 = bf16[256,4,512]{2,1,0:T(4,128)(2,1)} custom-call(bf16[256,4,4096]{2,1,0:T(4,128)(2,1)} %hid_in.1, bf16[4096,512]{1,0:T(8,128)(2,1)} %val_in.1, bf16[8,128,2048]{2,1,0:T(8,128)(2,1)} %bitcast.4, bf16[1024,512]{1,0:T(8,128)(2,1)} %bitcast.5, s32[1024,128]{1,0:T(8,128)} %broadcast_subtract_fusion.key), custom_call_target="tpu_custom_call" | custom-call | flops 30000001024 | bytes 20000000 | tf_op jit(solution)/shard_map/pallas_call | solution.py:465
  178.5 2.6 %copy.7 = bf16[256,4,512]{2,1,0:T(4,128)(2,1)} copy(bf16[256,4,512]{2,1,0:T(4,128)(2,1)} %shard_map.55) | data formatting | bytes 2097152
  (1 shorter events, 0.0 us)
